TPU v7x, 32 devices: a whole 2x2x4 slice. The times are simulated.
32 devices in a mesh: seg: 8 (over z, x), col: 4 (over y, core).
Axes of the slice: x: 2, y: 2, z: 4, core: 2. Of those that a mesh axis runs over, the one named last changes fastest.
Arguments:
- margin: float32 [1536, 1536], P('seg'), as said below
- leaf_factor: float32 [1536, 1536], P('seg', 'col'), as said below
Outputs:
- factor: float32 [1536, 1536], P('seg', 'col')
- errors: float32 [2], replicated
Inputs may be any that keep to these rules, and one draw needn't show every extreme that they name: margin is symmetric and positive definite; entries with |row - column| >= 2048 are zero. leaf_factor is zero outside the four diagonal blocks of 384 rows and columns; each block is upper triangular.
All inputs are finite; a program needn't handle non-finite values.
Results may differ from a plain program's by a relative error of at most 0.00005.
Values sent between devices are 32-bit elements; how exact they have to be, the bound alone decides.
A program may use at most 64 MiB of HBM per device.

v0:
```python
import jax
import jax.numpy as jnp
from jax import lax
from jax.sharding import PartitionSpec as P


def contract(left, right, left_dim, right_dim):
    return lax.dot_general(
        left,
        right,
        (((left_dim,), (right_dim,)), ((), ())),
        precision=lax.Precision.HIGHEST,
        preferred_element_type=jnp.float32,
    )


def refine(margin_rows, factor, identity):
    columns = margin_rows
    applied = contract(columns, lax.all_gather(factor, "seg", axis=0, tiled=True), 1, 0)
    factor_rows = lax.all_gather(factor, "col", axis=1, tiled=True)
    columns = factor_rows
    coupling = lax.psum_scatter(
        contract(columns, applied, 0, 0), "seg", scatter_dimension=0, tiled=True
    )
    defect = identity - coupling
    columns = factor_rows
    update = contract(columns, lax.all_gather(defect, "seg", axis=0, tiled=True), 1, 0)
    squares = jnp.sum(defect * defect)
    return (factor + 0.5 * update, squares)


def level_total(squares):
    return lax.psum(squares, ("seg", "col"))


def body(margin, leaf_factor):
    row_count, full_width = margin.shape
    col_count = leaf_factor.shape[1]
    row_ids = lax.axis_index("seg") * row_count + jnp.arange(row_count, dtype=jnp.int32)
    col_ids = lax.axis_index("col") * col_count + jnp.arange(col_count, dtype=jnp.int32)
    half_size = full_width // 2
    all_ids = jnp.arange(full_width, dtype=jnp.int32)
    same_half = row_ids[:, None] // half_size == all_ids[None, :] // half_size
    split_margin = jnp.where(same_half, margin, jnp.float32(0.0))
    identity = (row_ids[:, None] == col_ids[None, :]).astype(jnp.float32)
    middle, squares_low = refine(split_margin, leaf_factor, identity)
    total_low = level_total(squares_low)
    factor, squares_top = refine(margin, middle, identity)
    total_top = level_total(squares_top)
    errors = jnp.sqrt(jnp.stack([total_low, total_top]) / full_width)
    return (factor, errors)


def solution(mesh):
    return jax.shard_map(
        body,
        mesh=mesh,
        in_specs=(P("seg", None), P("seg", "col")),
        out_specs=(P("seg", "col"), P()),
        check_vma=False,
    )
```

profile of v0, /device:TPU:0, one launch (start us, length us, event | category | flops | bytes accessed | tf_op | source)
XLA Modules:
  0.0 428.0 jit_solution(13796848365405797715)
XLA Ops:
  7.2 0.0 all-gather.7.cloned.1.call-start
  7.2 0.7 all-gather.7.cloned.1.call-update
  7.9 0.0 all-gather.9.cloned.1.call-start
  7.9 0.7 all-gather.9.cloned.1.call-update
  8.6 0.0 reduce-scatter.7.cloned.1.call-start
  8.7 56.3 %all-gather.7.cloned.1.call-done = f32[1536,384]{1,0:T(8,128)} async-done(((f32[192,384]{1,0:T(8,128)}), f32[1536,384]{1,0:T(8,128)}) %all-gather.7.cloned.1.call-update) | async-done | bytes 2359312 | tf_op jit(solution)/shard_map/all_gather | solution.py:19
  65.0 4.2 fusion
  69.2 13.4 %all-gather.9.cloned.1.call-done = f32[192,1536]{1,0:T(8,128)} async-done(((f32[192,384]{1,0:T(8,128)}), f32[192,1536]{1,0:T(8,128)}) %all-gather.9.cloned.1.call-update) | async-done | bytes 1179664 | tf_op jit(solution)/shard_map/all_gather | solution.py:20
  82.6 3.3 convolution_bitcast_fusion
  85.9 2.0 copy.9
  87.9 0.0 reduce-scatter.7.cloned.1.call-update
  87.9 0.0 all-gather.11.cloned.1.call-start
  88.0 0.0 copy-start.2
  88.0 0.0 copy-start.4
  88.0 69.1 %reduce-scatter.7.cloned.1.call-done = f32[192,384]{1,0:T(8,128)} async-done(((f32[1536,384]{1,0:T(8,128)}), f32[192,384]{1,0:T(8,128)}) %reduce-scatter.7.cloned.1.call-update) | async-done | bytes 294928
  157.1 1.1 copy.10
  158.2 0.8 multiply_reduce_fusion.1
  159.0 0.9 copy.5
  159.9 0.0 all-gather.11.cloned.1.call-update
  159.9 0.0 all-gather.15.cloned.1.call-start
  159.9 51.2 %all-gather.11.cloned.1.call-done = f32[1536,384]{1,0:T(8,128)} async-done(((f32[192,384]{1,0:T(8,128)}), f32[1536,384]{1,0:T(8,128)}) %all-gather.11.cloned.1.call-update) | async-done | bytes 2359312 | tf_op jit(solution)/shard_map/all_gather | solution.py:27
  211.2 0.0 copy-done.2
  211.2 0.0 copy-done.4
  211.2 0.0 copy-start.1
  211.2 4.7 %fusion.5 = f32[192,384]{1,0:T(8,128)} fusion(f32[192,384]{1,0:T(8,128)S(1)} %copy-done.4, f32[1536,384]{1,0:T(8,128)} %all-gather.11.cloned.1.call-done, f32[192,1536]{1,0:T(8,128)S(1)} %copy-done.2), kind=kOutput, calls=%fused_computation.8 | convolution fusion | flops 1359101952 | bytes 4128768 | tf_op jit(solution)/shard_map/dot_general | solution.py:8
  215.9 0.0 all-gather.15.cloned.1.call-update
  215.9 0.0 all-gather.13.cloned.1.call-start
  216.0 0.5 all-gather.13.cloned.1.call-update
  216.5 0.2 reduce-scatter.9.cloned.1.call-start
  216.7 50.0 %all-gather.15.cloned.1.call-done = f32[1536,384]{1,0:T(8,128)} async-done(((f32[192,384]{1,0:T(8,128)}), f32[1536,384]{1,0:T(8,128)}) %all-gather.15.cloned.1.call-update) | async-done | bytes 2359312 | tf_op jit(solution)/shard_map/all_gather | solution.py:19
  266.7 0.0 copy-done.1
  266.7 5.5 %fusion.14 = f32[384,192]{1,0:T(8,128)S(1)} fusion(f32[1536,384]{1,0:T(8,128)} %all-gather.15.cloned.1.call-done, f32[192,1536]{1,0:T(8,128)S(1)} %copy-done.1), kind=kOutput, calls=%fused_computation.29 | convolution fusion | flops 1358954496 | bytes 3833856 | tf_op jit(solution)/shard_map/dot_general | solution.py:8
  272.2 12.5 %all-gather.13.cloned.1.call-done = f32[192,1536]{1,0:T(8,128)} async-done(((f32[192,384]{1,0:T(8,128)}), f32[192,1536]{1,0:T(8,128)}) %all-gather.13.cloned.1.call-update) | async-done | bytes 1179664 | tf_op jit(solution)/shard_map/all_gather | solution.py:20
  284.7 7.8 %fusion.15 = f32[1536,384]{1,0:T(8,128)} fusion(f32[192,1536]{1,0:T(8,128)} %all-gather.13.cloned.1.call-done, f32[384,192]{1,0:T(8,128)S(1)} %fusion.14), kind=kOutput, calls=%fused_computation.30 | convolution fusion | flops 1358954496 | bytes 3833856
  292.5 0.0 reduce-scatter.9.cloned.1.call-update
  292.5 0.0 copy-start
  292.5 0.0 copy-start.3
  292.5 0.0 all-gather.17.cloned.1.call-start
  292.6 69.2 %reduce-scatter.9.cloned.1.call-done = f32[192,384]{1,0:T(8,128)} async-done(((f32[1536,384]{1,0:T(8,128)}), f32[192,384]{1,0:T(8,128)}) %reduce-scatter.9.cloned.1.call-update) | async-done | bytes 294928
  361.7 1.1 copy.12
  362.9 0.8 multiply_reduce_fusion
  363.7 0.9 copy.7
  364.6 0.0 all-gather.17.cloned.1.call-update
  364.6 41.1 %all-reduce = (f32[1]{0:T(128)}, f32[1]{0:T(128)}) all-reduce(f32[1]{0:T(128)} %bitcast.3, f32[1]{0:T(128)} %bitcast.2), channel_id=1, replica_groups=mesh['seg'=8,'col'=4] {'seg','col'}, use_global_device_ids=true, to_apply=%region_5.6 | all-reduce | flops 2 | bytes 16 | tf_op jit(solution)/shard_map/psum | solution.py:33
  405.7 1.9 fusion.12
  407.6 9.0 %all-gather.17.cloned.1.call-done = f32[1536,384]{1,0:T(8,128)} async-done(((f32[192,384]{1,0:T(8,128)}), f32[1536,384]{1,0:T(8,128)}) %all-gather.17.cloned.1.call-update) | async-done | bytes 2359312 | tf_op jit(solution)/shard_map/all_gather | solution.py:27
  416.6 0.0 copy-done
  416.6 0.0 copy-done.3
  416.6 4.5 %fusion.3 = f32[192,384]{1,0:T(8,128)} fusion(f32[192,384]{1,0:T(8,128)S(1)} %copy-done, f32[192,1536]{1,0:T(8,128)S(1)} %copy-done.3, f32[1536,384]{1,0:T(8,128)} %all-gather.17.cloned.1.call-done), kind=kOutput, calls=%fused_computation.5 | convolution fusion | flops 1359101952 | bytes 4128768 | tf_op jit(solution)/shard_map/dot_general | solution.py:8
  (4 shorter events, 0.0 us)
Async XLA Ops:
  7.2 57.8 %all-gather.7.cloned.1.call-start = ((), (), s32[]{:S(2)}) async-start(), calls=%async_computation.2 | async-start | bytes 2654208 | tf_op jit(solution)/shard_map/all_gather | solution.py:19
  7.9 74.7 %all-gather.9.cloned.1.call-start = ((), (), s32[]{:S(2)}) async-start(), calls=%async_computation.3 | async-start | bytes 1474560 | tf_op jit(solution)/shard_map/all_gather | solution.py:20
  8.6 148.4 %reduce-scatter.7.cloned.1.call-start = ((), (), s32[]{:S(2)}) async-start(), calls=%async_computation.8 | async-start | bytes 2654208
  87.9 123.3 %all-gather.11.cloned.1.call-start = ((), (), s32[]{:S(2)}) async-start(), calls=%async_computation.4 | async-start | bytes 2654208 | tf_op jit(solution)/shard_map/all_gather | solution.py:27
  88.0 123.2 %copy-start.2 = (f32[192,1536]{1,0:T(8,128)S(1)}, f32[192,1536]{1,0:T(8,128)}, u32[]{:S(2)}) copy-start(f32[192,1536]{1,0:T(8,128)} %all-gather.9.cloned.1.call-done) | copy-start | bytes 3538948
  88.0 123.2 %copy-start.4 = (f32[192,384]{1,0:T(8,128)S(1)}, f32[192,384]{1,0:T(8,128)}, u32[]{:S(2)}) copy-start(f32[192,384]{1,0:T(8,128)} %param.3) | copy-start | bytes 884740
  159.9 106.8 %all-gather.15.cloned.1.call-start = ((), (), s32[]{:S(2)}) async-start(), calls=%async_computation.6 | async-start | bytes 2654208 | tf_op jit(solution)/shard_map/all_gather | solution.py:19
  211.2 55.5 %copy-start.1 = (f32[192,1536]{1,0:T(8,128)S(1)}, f32[192,1536]{1,0:T(8,128)}, u32[]{:S(2)}) copy-start(f32[192,1536]{1,0:T(8,128)} %param.2) | copy-start | bytes 3538948
  215.9 68.8 %all-gather.13.cloned.1.call-start = ((), (), s32[]{:S(2)}) async-start(), calls=%async_computation.5 | async-start | bytes 1474560 | tf_op jit(solution)/shard_map/all_gather | solution.py:20
  216.5 145.2 %reduce-scatter.9.cloned.1.call-start = ((), (), s32[]{:S(2)}) async-start(), calls=%async_computation.9 | async-start | bytes 2654208
  292.5 124.1 %copy-start = (f32[192,384]{1,0:T(8,128)S(1)}, f32[192,384]{1,0:T(8,128)}, u32[]{:S(2)}) copy-start(f32[192,384]{1,0:T(8,128)} %fusion.5) | copy-start | bytes 884740
  292.5 124.1 %copy-start.3 = (f32[192,1536]{1,0:T(8,128)S(1)}, f32[192,1536]{1,0:T(8,128)}, u32[]{:S(2)}) copy-start(f32[192,1536]{1,0:T(8,128)} %all-gather.13.cloned.1.call-done) | copy-start | bytes 3538948
  292.5 124.1 %all-gather.17.cloned.1.call-start = ((), (), s32[]{:S(2)}) async-start(), calls=%async_computation.7 | async-start | bytes 2654208 | tf_op jit(solution)/shard_map/all_gather | solution.py:27
Sparse Core Ops, SparseCore 0:
  10.2 54.7 all-gather.6
  66.5 15.9 all-gather.8
  88.0 69.0 reduce-scatter.6
  160.0 51.1 all-gather.10
  216.0 50.5 all-gather.14
  268.7 15.9 all-gather.12
  292.6 69.0 reduce-scatter.8
  364.7 51.8 all-gather.16
where the time goes:
time: 428 us
  waiting for transfers between devices  333 us (78%)
  blocking collectives  41.1 us (10%)
  matrix products  30 us (7%)
  between operations  14.2 us (3%)
  local copies, waits for them, and re-layouts  5.99 us (1%)
    unnamed x10, waiting for transfers between devices  140 us
    all_gather x2, waiting for transfers between devices, refine(): lax.all_gather(factor, 'seg', axis=0, tiled=True)  106 us
    all_gather x2, waiting for transfers between devices, refine(): lax.all_gather(defect, 'seg', axis=0, tiled=True)  60.3 us
    psum x1, blocking collectives, level_total(): return lax.psum(squares, ('seg', 'col'))  41.1 us
    all_gather x2, waiting for transfers between devices, refine(): factor_rows = lax.all_gather(factor, 'col', axis=1, tiled=True)  25.9 us
    dot_general x5, matrix products, contract(): lax.dot_general(left, right, (((left_dim,), (right_dim,)), ((), ())), pre...  22.3 us
  transfers between devices with their start and end apart: 8, of which 8 were waited for; matrix products, arithmetic and copies ran while one was open for 3% of the time, Pallas kernels for 0%

commit v1 on v0

v1 whole, which is shorter than its diff:
```python
import functools

import jax
import jax.numpy as jnp
from jax import lax
from jax.experimental import pallas as pl
from jax.experimental.pallas import tpu as pltpu
from jax.sharding import PartitionSpec as P

MESH = pl.DeviceIdType.MESH
F32 = jnp.float32
CHUNKS = 3
SENDS = 128


def dot(left, right, left_dim=1):
    return lax.dot_general(
        left,
        right,
        (((left_dim,), (0,)), ((), ())),
        precision=lax.Precision.HIGHEST,
        preferred_element_type=F32,
    )


def fold(values):
    rows, width = values.shape
    tall = jnp.sum(values.reshape(rows // 8, 8, width), axis=0)
    total = tall[:, :128]
    for start in range(128, width, 128):
        total = total + tall[:, start:start + 128]
    return total


def kernel(
    nseg, ncol, order,
    margin_ref, leaf_ref, out_ref, err_ref,
    sblk, lcol, lrow, part, rk, kcol, rp, rm, mb, eb, jb, sq1, sq2,
    send, lz_r, lx_r, lrow_r, rk_r, kz_r, kx_r, row_r, pair_r, m_r, e_r, q1_r, q2_r, local,
):
    rows, width = leaf_ref.shape
    nx = nseg // 4
    cq = ncol // 4
    hs, hc = nseg // 2, ncol // 2
    per = width // rows
    quarter = nx * rows
    step = rows // CHUNKS

    seg = lax.axis_index("seg")
    col = lax.axis_index("col")
    z, x = lax.div(seg, nx), lax.rem(seg, nx)
    qc = lax.div(col, cq)
    hseg, hcol = lax.div(z, 2), lax.div(qc, 2)
    diag = hseg == hcol
    mine = lax.rem(col, hc)
    half_col = col - mine

    pending = []
    used = [0]

    def true():
        return seg >= 0

    def push(cond, src, dst, rsem, to_seg, to_col):
        index = used[0]
        used[0] += 1
        copy = pltpu.make_async_remote_copy(
            src_ref=src, dst_ref=dst, send_sem=send.at[index], recv_sem=rsem,
            device_id=(to_seg, to_col), device_id_type=MESH,
        )
        if cond is None:
            copy.start()
        else:
            pl.when(cond)(copy.start)
        pending.append((cond, copy))

    def arrive(cond, dst, rsem):
        copy = pltpu.make_async_remote_copy(
            src_ref=dst, dst_ref=dst, send_sem=send.at[0], recv_sem=rsem,
            device_id=(seg, lax.rem(col + 1, ncol)), device_id_type=MESH,
        )
        if cond is None:
            copy.wait_recv()
        else:
            pl.when(cond)(copy.wait_recv)

    def other_x(d):
        return z * nx + lax.rem(x + d, nx)

    fetch = pltpu.make_async_copy(
        margin_ref.at[:, pl.ds(pl.multiple_of(qc * quarter, 128), quarter)], sblk, local.at[0]
    )
    fetch.start()
    owner = qc == z
    own_slot = lax.rem(col, cq)

    @pl.when(owner)
    def _():
        lcol[x] = leaf_ref[...]
        lrow[own_slot] = leaf_ref[...]

    barrier = pltpu.get_barrier_semaphore()
    for d in range(1, nseg):
        pl.semaphore_signal(barrier, inc=1, device_id=(lax.rem(seg + d, nseg), col), device_id_type=MESH)
    for d in range(1, ncol):
        pl.semaphore_signal(barrier, inc=1, device_id=(seg, lax.rem(col + d, ncol)), device_id_type=MESH)
    pl.semaphore_wait(barrier, nseg + ncol - 2)

    for j in range(CHUNKS):
        here = pl.ds(j * step, step)
        block = lcol.at[x, here]
        arrive(jnp.logical_not(owner), block, lz_r.at[j])
        push((z >= qc) & (z < 3), block, block, lz_r.at[j], seg + nx, col)
        push((z <= qc) & (z > 0), block, block, lz_r.at[j], seg - nx, col)
        for d in range(1, nx):
            push(None, block, block, lx_r.at[x, j], other_x(d), col)
    for d in range(1, ncol):
        push(owner, lrow.at[own_slot], lrow.at[own_slot], lrow_r.at[own_slot], seg, lax.rem(col + d, ncol))
    for d in range(1, nx):
        from_x = lax.rem(x + d, nx)
        for j in range(CHUNKS):
            arrive(None, lcol.at[from_x, pl.ds(j * step, step)], lx_r.at[from_x, j])
    fetch.wait()
    applied = dot(sblk[...], lcol[...].reshape(quarter, width))
    for k in range(cq):
        arrive(jnp.logical_not(owner & (own_slot == k)), lrow.at[k], lrow_r.at[k])
    for k in range(cq):
        piece = dot(lrow[k], applied, 0)
        part[pl.ds(k * per, per)] = piece.reshape(per, rows, width)
    for d in range(1, nx):
        push(None, part.at[lax.rem(x + d, nx)], rk.at[x], rk_r.at[x], other_x(d), col)
    total = part[x]
    for d in range(1, nx):
        from_x = lax.rem(x + d, nx)
        arrive(None, rk.at[from_x], rk_r.at[from_x])
        total = total + rk[from_x]
    kcol[seg] = total

    def spread(distance, up):
        origin = z - distance if up else z + distance
        valid = (origin >= 0) & (origin <= 3)
        wide = lax.div(origin, 2) == hcol
        same = lax.div(origin, 2) == hseg
        reached = valid & (wide | same)
        low = jnp.where(wide, 0, 2 * hseg)
        high = jnp.where(wide, 3, 2 * hseg + 1)
        slot = jnp.clip(origin, 0, 3) * nx + x
        plane = jnp.clip(origin, 0, 3)
        for j in range(CHUNKS):
            block = kcol.at[slot, pl.ds(j * step, step)]
            if distance:
                arrive(reached, block, kz_r.at[plane, j])
            if up or distance == 0:
                push(reached & (z < high), block, block, kz_r.at[plane, j], seg + nx, col)
            if not up or distance == 0:
                push(reached & (z > low), block, block, kz_r.at[plane, j], seg - nx, col)
            for d in range(1, nx):
                push(reached, block, block, kx_r.at[slot, j], other_x(d), col)

    def settle(distance, up):
        origin = z - distance if up else z + distance
        valid = (origin >= 0) & (origin <= 3)
        reached = valid & ((lax.div(origin, 2) == hcol) | (lax.div(origin, 2) == hseg))
        for d in range(1, nx):
            slot = jnp.clip(origin, 0, 3) * nx + lax.rem(x + d, nx)
            for j in range(CHUNKS):
                arrive(reached, kcol.at[slot, pl.ds(j * step, step)], kx_r.at[slot, j])

    spread(0, False)

    partner = lax.rem(col + hc, ncol)
    row_ids = seg * rows + lax.broadcasted_iota(jnp.int32, (rows, width), 0)
    col_ids = col * width + lax.broadcasted_iota(jnp.int32, (rows, width), 1)
    identity = (row_ids == col_ids).astype(F32)

    def siblings(cond, buf, rsem, which):
        for d in range(1, hc):
            push(cond, buf.at[mine], buf.at[mine], rsem.at[which, mine], seg, half_col + lax.rem(mine + d, hc))

    def from_siblings(cond, buf, rsem, which):
        for d in range(1, hc):
            k = lax.rem(mine + d, hc)
            arrive(cond, buf.at[k], rsem.at[which, k])

    @pl.when(diag)
    def _():
        own = kcol[seg]
        defect = identity - own
        sq1[seg, pl.ds(0, 8)] = fold(defect * defect)
        rp[mine] = 1.5 * identity - 0.5 * own

    @pl.when(jnp.logical_not(diag))
    def _():
        sq1[seg, pl.ds(0, 8)] = jnp.zeros((8, 128), F32)

    push(diag, rp.at[mine], rp.at[mine], pair_r.at[0], seg, partner)
    siblings(diag, rp, row_r, 0)

    spread(1, True)
    spread(1, False)
    spread(2, True)
    spread(2, False)
    spread(3, True)
    spread(3, False)
    off = jnp.logical_not(diag)
    arrive(off, rp.at[mine], pair_r.at[0])
    siblings(off, rp, row_r, 0)

    settle(0, False)

    @pl.when(diag)
    def _():
        near = kcol[pl.ds(z * nx, nx)].reshape(quarter, width)
        update = jnp.zeros((rows, width), F32)
        for k in range(cq):
            update = update + dot(lrow[k], near[k * width:(k + 1) * width])
        mb[mine] = 1.5 * leaf_ref[...] - 0.5 * update

    siblings(diag, mb, m_r, 0)
    settle(1, True)
    settle(1, False)
    from_siblings(diag, mb, m_r, 0)

    def product(buf, half):
        total = None
        for k in range(hc):
            term = dot(buf[k], kcol[pl.ds(half * hs + k * per, per)].reshape(width, width))
            total = term if total is None else total + term
        return total

    @pl.when(diag)
    def _():
        rm[mine] = 1.5 * mb[mine] - 0.5 * product(mb, hseg)

    push(diag, rm.at[mine], rm.at[mine], pair_r.at[1], seg, partner)
    siblings(diag, rm, row_r, 1)

    from_siblings(None, rp, row_r, 0)
    eb[mine] = product(rp, hseg)
    siblings(None, eb, e_r, 0)

    arrive(off, rm.at[mine], pair_r.at[1])
    siblings(off, rm, row_r, 1)
    from_siblings(None, rm, row_r, 1)
    jb[mine] = product(rm, hseg)
    siblings(None, jb, e_r, 1)

    settle(2, True)
    settle(2, False)
    settle(3, True)
    settle(3, False)
    from_siblings(None, eb, e_r, 0)
    coupling = 1.5 * eb[mine] - 0.5 * product(eb, hcol)
    defect = identity - coupling
    sq1[seg, pl.ds(8, 8)] = fold(defect * defect)
    for d in range(1, nseg):
        push(None, sq1.at[seg], sq1.at[seg], q1_r.at[seg], lax.rem(seg + d, nseg), col)

    from_siblings(None, jb, e_r, 1)
    tail = 1.5 * jb[mine] - 0.5 * product(jb, hcol)

    @pl.when(diag)
    def _():
        out_ref[...] = 1.5 * mb[mine] - 0.5 * tail

    @pl.when(off)
    def _():
        out_ref[...] = -0.5 * tail

    for d in range(1, nseg):
        k = lax.rem(seg + d, nseg)
        arrive(None, sq1.at[k], q1_r.at[k])
    sq2[col] = jnp.sum(sq1[...], axis=0)
    for d in range(1, ncol):
        push(None, sq2.at[col], sq2.at[col], q2_r.at[col], seg, lax.rem(col + d, ncol))
    for d in range(1, ncol):
        k = lax.rem(col + d, ncol)
        arrive(None, sq2.at[k], q2_r.at[k])
    tiles = jnp.sum(sq2[...], axis=0)
    for level in range(2):
        amount = jnp.sum(tiles[8 * level:8 * level + 8], axis=(0, 1), keepdims=True)
        err_ref[pl.ds(level, 1)] = jnp.broadcast_to(jnp.sqrt(amount / order), (1, 128))

    for cond, copy in pending:
        if cond is None:
            copy.wait_send()
        else:
            pl.when(cond)(copy.wait_send)


def body(nseg, ncol, margin, leaf_factor):
    rows, width = leaf_factor.shape
    order = margin.shape[1]
    nx, cq, hc = nseg // 4, ncol // 4, ncol // 2
    dma = pltpu.SemaphoreType.DMA
    factor, errors = pl.pallas_call(
        functools.partial(kernel, nseg, ncol, order),
        out_shape=(
            jax.ShapeDtypeStruct((rows, width), F32),
            jax.ShapeDtypeStruct((2, 128), F32),
        ),
        in_specs=[pl.BlockSpec(memory_space=pl.ANY), pl.BlockSpec(memory_space=pltpu.VMEM)],
        out_specs=(pl.BlockSpec(memory_space=pltpu.VMEM),) * 2,
        scratch_shapes=[
            pltpu.VMEM((rows, nx * rows), F32),
            pltpu.VMEM((nx, rows, width), F32),
            pltpu.VMEM((cq, rows, width), F32),
            pltpu.VMEM((nx, rows, width), F32),
            pltpu.VMEM((nx, rows, width), F32),
            pltpu.VMEM((nseg, rows, width), F32),
            pltpu.VMEM((hc, rows, width), F32),
            pltpu.VMEM((hc, rows, width), F32),
            pltpu.VMEM((hc, rows, width), F32),
            pltpu.VMEM((hc, rows, width), F32),
            pltpu.VMEM((hc, rows, width), F32),
            pltpu.VMEM((nseg, 16, 128), F32),
            pltpu.VMEM((ncol, 16, 128), F32),
            dma((SENDS + 16 * nseg,)),
            dma((CHUNKS,)),
            dma((nx, CHUNKS)),
            dma((cq,)),
            dma((nx,)),
            dma((4, CHUNKS)),
            dma((nseg, CHUNKS)),
            dma((2, hc)),
            dma((2,)),
            dma((1, hc)),
            dma((2, hc)),
            dma((nseg,)),
            dma((ncol,)),
            dma((1,)),
        ],
        compiler_params=pltpu.CompilerParams(
            collective_id=0, has_side_effects=True, vmem_limit_bytes=56 * 1024 * 1024
        ),
    )(margin, leaf_factor)
    return factor, errors[:, 0]


def solution(mesh):
    return jax.shard_map(
        functools.partial(body, mesh.shape["seg"], mesh.shape["col"]),
        mesh=mesh,
        in_specs=(P("seg", None), P("seg", "col")),
        out_specs=(P("seg", "col"), P()),
        check_vma=False,
    )
```

time: 428 us -> 75.7 us (0.18)
  waiting for transfers between devices: 333 us -> 0 us
  Pallas kernels: 0 us -> 71.9 us
  blocking collectives: 41.1 us -> 0 us
  matrix products: 30 us -> 0 us
  between operations: 14.2 us -> 0.64 us
    all_gather x6 -> x0, waiting for transfers between devices: 192 us -> none  [the longest x2 106 us: refine(): lax.all_gather(factor, 'seg', axis=0, tiled=True)]
    unnamed x10 -> x0, waiting for transfers between devices: 140 us -> none
    pallas_call x0 -> x1, Pallas kernels: none -> 71.9 us  [body(): pl.pallas_call(functools.partial(kernel, nseg, ncol, order), out_shape=(j...]
    psum x1 -> x0, blocking collectives: 41.1 us -> none  [level_total(): return lax.psum(squares, ('seg', 'col'))]
    dot_general x5 -> x0, matrix products: 22.3 us -> none  [contract(): lax.dot_general(left, right, (((left_dim,), (right_dim,)), ((), ())), pre...]
    unnamed x1 -> x0, matrix products: 7.77 us -> none
  transfers between devices with their start and end apart: 8 -> 0, of which waited for: 8 -> 0; matrix products, arithmetic and copies ran while one was open for 3% -> 0% of each run, Pallas kernels for 0% -> 0%
where the time goes in v1:
time: 75.7 us; the launch traced here: 75.5 us
  Pallas kernels  71.9 us (95%)
  local copies, waits for them, and re-layouts  2.98 us (4%)
    pallas_call x1, Pallas kernels, body(): pl.pallas_call(functools.partial(kernel, nseg, ncol, order), out_shape=(j...  71.9 us
    unnamed x1, local copies, waits for them, and re-layouts  1.69 us

profile of v1, /device:TPU:0, one launch (start us, length us, event | category | flops | bytes accessed | tf_op | source)
XLA Modules:
  0.0 75.5 jit_solution(15589726368777480523)
XLA Ops:
  0.6 71.9 %shard_map.41 = (f32[192,384]{1,0:T(8,128)}, f32[2,128]{1,0:T(2,128)}) custom-call(f32[192,1536]{1,0:T(8,128)} %margin_ref.1, f32[192,384]{1,0:T(8,128)} %leaf_ref.1), custom_call_target="tpu_custom_call" | custom-call | tf_op jit(solution)/shard_map/pallas_call | solution.py:296
  72.5 1.3 %slice_reduce_fusion = f32[2]{0:T(128)} fusion(f32[2,128]{1,0:T(2,128)} %get-tuple-element.5), kind=kLoop, calls=%fused_computation | loop fusion | bytes 16 | tf_op jit(solution)/shard_map/slice | solution.py:337
  73.8 1.7 %copy.5 = f32[192,384]{1,0:T(8,128)} copy(f32[192,384]{1,0:T(8,128)} %get-tuple-element.8) | data formatting | bytes 589824

commit v2 on v1

--- a/solution.py
+++ b/solution.py
@@ -23,6 +23,20 @@
     )
 
 
+def parts(values):
+    high = values.astype(jnp.bfloat16)
+    return high, (values - high.astype(F32)).astype(jnp.bfloat16)
+
+
+def dot3(left, right):
+    rows = left.shape[0]
+    left_high, left_low = parts(left)
+    right_high, right_low = parts(right)
+    both = jnp.dot(jnp.concatenate([left_high, left_low], axis=0), right_high, preferred_element_type=F32)
+    rest = jnp.dot(left_high, right_low, preferred_element_type=F32)
+    return both[:rows] + (both[rows:] + rest)
+
+
 def fold(values):
     rows, width = values.shape
     tall = jnp.sum(values.reshape(rows // 8, 8, width), axis=0)
@@ -35,8 +49,8 @@
 def kernel(
     nseg, ncol, order,
     margin_ref, leaf_ref, out_ref, err_ref,
-    sblk, lcol, lrow, part, rk, kcol, rp, rm, mb, eb, jb, sq1, sq2,
-    send, lz_r, lx_r, lrow_r, rk_r, kz_r, kx_r, row_r, pair_r, m_r, e_r, q1_r, q2_r, local,
+    sblk, lcol, lrow, part, rk, ub, kcol, rp, rm, mb, eb, jb, sq1, sq2,
+    send, lz_r, lx_r, lrow_r, rk_r, ub_r, kz_r, kx_r, row_r, pair_r, m_r, e_r, q1_r, q2_r, local,
 ):
     rows, width = leaf_ref.shape
     nx = nseg // 4
@@ -88,7 +102,7 @@
         return z * nx + lax.rem(x + d, nx)
 
     fetch = pltpu.make_async_copy(
-        margin_ref.at[:, pl.ds(pl.multiple_of(qc * quarter, 128), quarter)], sblk, local.at[0]
+        margin_ref.at[:, pl.ds(pl.multiple_of(col * width, 128), width)], sblk, local.at[0]
     )
     fetch.start()
     owner = qc == z
@@ -106,35 +120,69 @@
         pl.semaphore_signal(barrier, inc=1, device_id=(seg, lax.rem(col + d, ncol)), device_id_type=MESH)
     pl.semaphore_wait(barrier, nseg + ncol - 2)
 
+    mate = col + 1 - 2 * lax.rem(col, 2)
     for j in range(CHUNKS):
         here = pl.ds(j * step, step)
-        block = lcol.at[x, here]
+        for k in range(cq):
+            home = z * cq + k
+            lead = lax.rem(col, 2) == lax.rem(home, 2)
+            block = lrow.at[k, here]
+            for d in range(2, ncol, 2):
+                push(col == home, block, block, lrow_r.at[k, j], seg, lax.rem(col + d, ncol))
+            arrive(lead & (col != home), block, lrow_r.at[k, j])
+            push(lead, block, block, lrow_r.at[k, j], seg, mate)
+    for j in range(CHUNKS):
+        block = lcol.at[x, pl.ds(j * step, step)]
+        push(owner & (z < 3), block, block, lz_r.at[j], seg + nx, col)
+        push(owner & (z > 0), block, block, lz_r.at[j], seg - nx, col)
+    fetch.wait()
+    for j in range(CHUNKS):
+        for k in range(cq):
+            lead = lax.rem(col, 2) == lax.rem(z * cq + k, 2)
+            arrive(jnp.logical_not(lead), lrow.at[k, pl.ds(j * step, step)], lrow_r.at[k, j])
+    for k in range(cq):
+        piece = dot(lrow[k], sblk[...], 0)
+        part[pl.ds(k * per, per)] = piece.reshape(per, rows, width)
+    for j in range(CHUNKS):
+        here = pl.ds(j * step, step)
+        for d in range(1, nx):
+            to_x = jnp.minimum(x + d, nx - 1)
+            push(x + d < nx, part.at[to_x, here], rk.at[x, here], rk_r.at[x, j], z * nx + to_x, col)
+    for j in range(CHUNKS):
+        block = lcol.at[x, pl.ds(j * step, step)]
         arrive(jnp.logical_not(owner), block, lz_r.at[j])
-        push((z >= qc) & (z < 3), block, block, lz_r.at[j], seg + nx, col)
-        push((z <= qc) & (z > 0), block, block, lz_r.at[j], seg - nx, col)
+        push((z > qc) & (z < 3), block, block, lz_r.at[j], seg + nx, col)
+        push((z < qc) & (z > 0), block, block, lz_r.at[j], seg - nx, col)
         for d in range(1, nx):
             push(None, block, block, lx_r.at[x, j], other_x(d), col)
-    for d in range(1, ncol):
-        push(owner, lrow.at[own_slot], lrow.at[own_slot], lrow_r.at[own_slot], seg, lax.rem(col + d, ncol))
     for d in range(1, nx):
         from_x = lax.rem(x + d, nx)
         for j in range(CHUNKS):
             arrive(None, lcol.at[from_x, pl.ds(j * step, step)], lx_r.at[from_x, j])
-    fetch.wait()
-    applied = dot(sblk[...], lcol[...].reshape(quarter, width))
-    for k in range(cq):
-        arrive(jnp.logical_not(owner & (own_slot == k)), lrow.at[k], lrow_r.at[k])
-    for k in range(cq):
-        piece = dot(lrow[k], applied, 0)
-        part[pl.ds(k * per, per)] = piece.reshape(per, rows, width)
-    for d in range(1, nx):
-        push(None, part.at[lax.rem(x + d, nx)], rk.at[x], rk_r.at[x], other_x(d), col)
-    total = part[x]
-    for d in range(1, nx):
-        from_x = lax.rem(x + d, nx)
-        arrive(None, rk.at[from_x], rk_r.at[from_x])
-        total = total + rk[from_x]
-    kcol[seg] = total
+
+    def form(j):
+        here = pl.ds(j * step, step)
+        ub[own_slot, here] = part[x, here]
+        for d in range(1, nx):
+            from_x = jnp.maximum(x - d, 0)
+            arrive(x >= d, rk.at[from_x, here], rk_r.at[from_x, j])
+
+            @pl.when(x >= d)
+            def _():
+                ub[own_slot, here] += rk[from_x, here]
+
+        first = col - own_slot
+        for d in range(1, cq):
+            block = ub.at[own_slot, here]
+            push(None, block, block, ub_r.at[own_slot, j], seg, first + lax.rem(own_slot + d, cq))
+        for d in range(1, cq):
+            k = lax.rem(own_slot + d, cq)
+            arrive(None, ub.at[k, here], ub_r.at[k, j])
+        total = None
+        for k in range(cq):
+            term = dot(ub[k, here], lcol[pl.ds(k * per, per)].reshape(width, width))
+            total = term if total is None else total + term
+        kcol[seg, here] = total
 
     def spread(distance, up):
         origin = z - distance if up else z + distance
@@ -148,6 +196,8 @@
         plane = jnp.clip(origin, 0, 3)
         for j in range(CHUNKS):
             block = kcol.at[slot, pl.ds(j * step, step)]
+            if distance == 0:
+                form(j)
             if distance:
                 arrive(reached, block, kz_r.at[plane, j])
             if up or distance == 0:
@@ -213,7 +263,7 @@
         near = kcol[pl.ds(z * nx, nx)].reshape(quarter, width)
         update = jnp.zeros((rows, width), F32)
         for k in range(cq):
-            update = update + dot(lrow[k], near[k * width:(k + 1) * width])
+            update = update + dot3(lrow[k], near[k * width:(k + 1) * width])
         mb[mine] = 1.5 * leaf_ref[...] - 0.5 * update
 
     siblings(diag, mb, m_r, 0)
@@ -224,7 +274,7 @@
     def product(buf, half):
         total = None
         for k in range(hc):
-            term = dot(buf[k], kcol[pl.ds(half * hs + k * per, per)].reshape(width, width))
+            term = dot3(buf[k], kcol[pl.ds(half * hs + k * per, per)].reshape(width, width))
             total = term if total is None else total + term
         return total
 
@@ -279,7 +329,7 @@
     tiles = jnp.sum(sq2[...], axis=0)
     for level in range(2):
         amount = jnp.sum(tiles[8 * level:8 * level + 8], axis=(0, 1), keepdims=True)
-        err_ref[pl.ds(level, 1)] = jnp.broadcast_to(jnp.sqrt(amount / order), (1, 128))
+        err_ref[level] = jnp.sqrt(amount / order)[0, 0]
 
     for cond, copy in pending:
         if cond is None:
@@ -297,16 +347,17 @@
         functools.partial(kernel, nseg, ncol, order),
         out_shape=(
             jax.ShapeDtypeStruct((rows, width), F32),
-            jax.ShapeDtypeStruct((2, 128), F32),
+            jax.ShapeDtypeStruct((2,), F32),
         ),
         in_specs=[pl.BlockSpec(memory_space=pl.ANY), pl.BlockSpec(memory_space=pltpu.VMEM)],
-        out_specs=(pl.BlockSpec(memory_space=pltpu.VMEM),) * 2,
+        out_specs=(pl.BlockSpec(memory_space=pltpu.VMEM), pl.BlockSpec(memory_space=pltpu.SMEM)),
         scratch_shapes=[
-            pltpu.VMEM((rows, nx * rows), F32),
+            pltpu.VMEM((rows, width), F32),
             pltpu.VMEM((nx, rows, width), F32),
             pltpu.VMEM((cq, rows, width), F32),
             pltpu.VMEM((nx, rows, width), F32),
             pltpu.VMEM((nx, rows, width), F32),
+            pltpu.VMEM((cq, rows, width), F32),
             pltpu.VMEM((nseg, rows, width), F32),
             pltpu.VMEM((hc, rows, width), F32),
             pltpu.VMEM((hc, rows, width), F32),
@@ -318,8 +369,9 @@
             dma((SENDS + 16 * nseg,)),
             dma((CHUNKS,)),
             dma((nx, CHUNKS)),
-            dma((cq,)),
-            dma((nx,)),
+            dma((cq, CHUNKS)),
+            dma((nx, CHUNKS)),
+            dma((cq, CHUNKS)),
             dma((4, CHUNKS)),
             dma((nseg, CHUNKS)),
             dma((2, hc)),
@@ -334,7 +386,7 @@
             collective_id=0, has_side_effects=True, vmem_limit_bytes=56 * 1024 * 1024
         ),
     )(margin, leaf_factor)
-    return factor, errors[:, 0]
+    return factor, errors
 
 
 def solution(mesh):

time: 75.7 us -> 71.5 us (0.945)
  Pallas kernels: 71.9 us -> 67.8 us
    pallas_call x1, Pallas kernels: 71.9 us -> 67.8 us  [body(): pl.pallas_call(functools.partial(kernel, nseg, ncol, order), out_shape=(j...]
    slice x1 -> x0, local copies, waits for them, and re-layouts: 1.29 us -> none  [body(): return (factor, errors[:, 0])]
    unnamed x1 -> x2, local copies, waits for them, and re-layouts: 1.69 us -> 2.88 us
where the time goes in v2:
time: 71.5 us; the launch traced here: 71.3 us
  Pallas kernels  67.8 us (95%)
  local copies, waits for them, and re-layouts  2.88 us (4%)
    pallas_call x1, Pallas kernels, body(): pl.pallas_call(functools.partial(kernel, nseg, ncol, order), out_shape=(j...  67.8 us
    unnamed x2, local copies, waits for them, and re-layouts  2.88 us

profile of v2, /device:TPU:0, one launch (start us, length us, event | category | flops | bytes accessed | tf_op | source)
XLA Modules:
  0.0 71.3 jit_solution(11261652204599998753)
XLA Ops:
  0.6 67.8 %shard_map.41 = (f32[192,384]{1,0:T(8,128)}, f32[2]{0:T(128)}) custom-call(f32[192,1536]{1,0:T(8,128)} %margin_ref.1, f32[192,384]{1,0:T(8,128)} %leaf_ref.1), custom_call_target="tpu_custom_call" | custom-call | tf_op jit(solution)/shard_map/pallas_call | solution.py:346
  68.4 1.7 %copy.6 = f32[192,384]{1,0:T(8,128)} copy(f32[192,384]{1,0:T(8,128)} %get-tuple-element.4) | data formatting | bytes 589824
  70.1 1.2 %copy.7 = f32[2]{0:T(128)} copy(f32[2]{0:T(128)} %get-tuple-element.5) | data formatting | bytes 16

commit v3 on v2

--- a/solution.py
+++ b/solution.py
@@ -131,10 +131,18 @@
                 push(col == home, block, block, lrow_r.at[k, j], seg, lax.rem(col + d, ncol))
             arrive(lead & (col != home), block, lrow_r.at[k, j])
             push(lead, block, block, lrow_r.at[k, j], seg, mate)
-    for j in range(CHUNKS):
-        block = lcol.at[x, pl.ds(j * step, step)]
-        push(owner & (z < 3), block, block, lz_r.at[j], seg + nx, col)
-        push(owner & (z > 0), block, block, lz_r.at[j], seg - nx, col)
+    near = (z - qc <= 1) & (qc - z <= 1)
+
+    def pass_on(chosen):
+        for j in range(CHUNKS):
+            block = lcol.at[x, pl.ds(j * step, step)]
+            arrive(chosen & jnp.logical_not(owner), block, lz_r.at[j])
+            push(chosen & (z >= qc) & (z < 3), block, block, lz_r.at[j], seg + nx, col)
+            push(chosen & (z <= qc) & (z > 0), block, block, lz_r.at[j], seg - nx, col)
+            for d in range(1, nx):
+                push(chosen, block, block, lx_r.at[x, j], other_x(d), col)
+
+    pass_on(near)
     fetch.wait()
     for j in range(CHUNKS):
         for k in range(cq):
@@ -148,13 +156,7 @@
         for d in range(1, nx):
             to_x = jnp.minimum(x + d, nx - 1)
             push(x + d < nx, part.at[to_x, here], rk.at[x, here], rk_r.at[x, j], z * nx + to_x, col)
-    for j in range(CHUNKS):
-        block = lcol.at[x, pl.ds(j * step, step)]
-        arrive(jnp.logical_not(owner), block, lz_r.at[j])
-        push((z > qc) & (z < 3), block, block, lz_r.at[j], seg + nx, col)
-        push((z < qc) & (z > 0), block, block, lz_r.at[j], seg - nx, col)
-        for d in range(1, nx):
-            push(None, block, block, lx_r.at[x, j], other_x(d), col)
+    pass_on(jnp.logical_not(near))
     for d in range(1, nx):
         from_x = lax.rem(x + d, nx)
         for j in range(CHUNKS):
@@ -184,7 +186,7 @@
             total = term if total is None else total + term
         kcol[seg, here] = total
 
-    def spread(distance, up):
+    def spread(distance, up, j):
         origin = z - distance if up else z + distance
         valid = (origin >= 0) & (origin <= 3)
         wide = lax.div(origin, 2) == hcol
@@ -192,31 +194,43 @@
         reached = valid & (wide | same)
         low = jnp.where(wide, 0, 2 * hseg)
         high = jnp.where(wide, 3, 2 * hseg + 1)
-        slot = jnp.clip(origin, 0, 3) * nx + x
         plane = jnp.clip(origin, 0, 3)
-        for j in range(CHUNKS):
-            block = kcol.at[slot, pl.ds(j * step, step)]
-            if distance == 0:
-                form(j)
-            if distance:
-                arrive(reached, block, kz_r.at[plane, j])
-            if up or distance == 0:
-                push(reached & (z < high), block, block, kz_r.at[plane, j], seg + nx, col)
-            if not up or distance == 0:
-                push(reached & (z > low), block, block, kz_r.at[plane, j], seg - nx, col)
-            for d in range(1, nx):
-                push(reached, block, block, kx_r.at[slot, j], other_x(d), col)
-
-    def settle(distance, up):
+        slot = plane * nx + x
+        block = kcol.at[slot, pl.ds(j * step, step)]
+        if distance:
+            arrive(reached, block, kz_r.at[plane, j])
+        if up or distance == 0:
+            push(reached & (z < high), block, block, kz_r.at[plane, j], seg + nx, col)
+        if not up or distance == 0:
+            push(reached & (z > low), block, block, kz_r.at[plane, j], seg - nx, col)
+        if distance < 2:
+            across = None if distance == 0 else reached & jnp.logical_not(same)
+        else:
+            across = reached
+        for d in range(1, nx):
+            push(across, block, block, kx_r.at[slot, j], other_x(d), col)
+
+    def settle(distance, up, j, inside):
         origin = z - distance if up else z + distance
         valid = (origin >= 0) & (origin <= 3)
-        reached = valid & ((lax.div(origin, 2) == hcol) | (lax.div(origin, 2) == hseg))
+        same = lax.div(origin, 2) == hseg
+        wide = lax.div(origin, 2) == hcol
+        reached = valid & (same if inside else wide & jnp.logical_not(same))
         for d in range(1, nx):
             slot = jnp.clip(origin, 0, 3) * nx + lax.rem(x + d, nx)
-            for j in range(CHUNKS):
-                arrive(reached, kcol.at[slot, pl.ds(j * step, step)], kx_r.at[slot, j])
-
-    spread(0, False)
+            arrive(reached, kcol.at[slot, pl.ds(j * step, step)], kx_r.at[slot, j])
+
+    def relay(j):
+        sibling = 2 * hseg + 1 - lax.rem(z, 2)
+        for d in range(1, nx):
+            slot = z * nx + lax.rem(x + d, nx)
+            block = kcol.at[slot, pl.ds(j * step, step)]
+            arrive(None, block, kx_r.at[slot, j])
+            push(None, block, block, kx_r.at[slot, j], sibling * nx + x, col)
+
+    for j in range(CHUNKS):
+        form(j)
+        spread(0, False, j)
 
     partner = lax.rem(col + hc, ncol)
     row_ids = seg * rows + lax.broadcasted_iota(jnp.int32, (rows, width), 0)
@@ -246,29 +260,29 @@
     push(diag, rp.at[mine], rp.at[mine], pair_r.at[0], seg, partner)
     siblings(diag, rp, row_r, 0)
 
-    spread(1, True)
-    spread(1, False)
-    spread(2, True)
-    spread(2, False)
-    spread(3, True)
-    spread(3, False)
     off = jnp.logical_not(diag)
+    for j in range(CHUNKS):
+        spread(1, True, j)
+        spread(1, False, j)
+    for j in range(CHUNKS):
+        relay(j)
+        spread(2, True, j)
+        spread(2, False, j)
     arrive(off, rp.at[mine], pair_r.at[0])
     siblings(off, rp, row_r, 0)
 
-    settle(0, False)
-
     @pl.when(diag)
     def _():
-        near = kcol[pl.ds(z * nx, nx)].reshape(quarter, width)
+        plane = kcol[pl.ds(z * nx, nx)].reshape(quarter, width)
         update = jnp.zeros((rows, width), F32)
         for k in range(cq):
-            update = update + dot3(lrow[k], near[k * width:(k + 1) * width])
+            update = update + dot3(lrow[k], plane[k * width:(k + 1) * width])
         mb[mine] = 1.5 * leaf_ref[...] - 0.5 * update
 
     siblings(diag, mb, m_r, 0)
-    settle(1, True)
-    settle(1, False)
+    for j in range(CHUNKS):
+        settle(1, True, j, True)
+        settle(1, False, j, True)
     from_siblings(diag, mb, m_r, 0)
 
     def product(buf, half):
@@ -288,6 +302,9 @@
     from_siblings(None, rp, row_r, 0)
     eb[mine] = product(rp, hseg)
     siblings(None, eb, e_r, 0)
+    for j in range(CHUNKS):
+        spread(3, True, j)
+        spread(3, False, j)
 
     arrive(off, rm.at[mine], pair_r.at[1])
     siblings(off, rm, row_r, 1)
@@ -295,10 +312,10 @@
     jb[mine] = product(rm, hseg)
     siblings(None, jb, e_r, 1)
 
-    settle(2, True)
-    settle(2, False)
-    settle(3, True)
-    settle(3, False)
+    for distance in (1, 2, 3):
+        for j in range(CHUNKS):
+            settle(distance, True, j, False)
+            settle(distance, False, j, False)
     from_siblings(None, eb, e_r, 0)
     coupling = 1.5 * eb[mine] - 0.5 * product(eb, hcol)
     defect = identity - coupling

time: 71.5 us -> 74.8 us (1.046)
  Pallas kernels: 67.8 us -> 70.9 us
    pallas_call x1, Pallas kernels: 67.8 us -> 70.9 us  [body(): pl.pallas_call(functools.partial(kernel, nseg, ncol, order), out_shape=(j...]
where the time goes in v3:
time: 74.8 us; the launch traced here: 74.4 us
  Pallas kernels  70.9 us (95%)
  local copies, waits for them, and re-layouts  2.88 us (4%)
    pallas_call x1, Pallas kernels, body(): pl.pallas_call(functools.partial(kernel, nseg, ncol, order), out_shape=(j...  70.9 us
    unnamed x2, local copies, waits for them, and re-layouts  2.88 us

profile of v3, /device:TPU:0, one launch (start us, length us, event | category | flops | bytes accessed | tf_op | source)
XLA Modules:
  0.0 74.4 jit_solution(5902007080315821963)
XLA Ops:
  0.6 70.9 %shard_map.41 = (f32[192,384]{1,0:T(8,128)}, f32[2]{0:T(128)}) custom-call(f32[192,1536]{1,0:T(8,128)} %margin_ref.1, f32[192,384]{1,0:T(8,128)} %leaf_ref.1), custom_call_target="tpu_custom_call" | custom-call | tf_op jit(solution)/shard_map/pallas_call | solution.py:363
  71.5 1.7 %copy.6 = f32[192,384]{1,0:T(8,128)} copy(f32[192,384]{1,0:T(8,128)} %get-tuple-element.4) | data formatting | bytes 589824
  73.2 1.2 %copy.7 = f32[2]{0:T(128)} copy(f32[2]{0:T(128)} %get-tuple-element.5) | data formatting | bytes 16

commit v4 on v3

--- a/solution.py
+++ b/solution.py
@@ -10,6 +10,7 @@
 MESH = pl.DeviceIdType.MESH
 F32 = jnp.float32
 CHUNKS = 3
+RELAYED = 1
 SENDS = 128
 
 
@@ -50,7 +51,7 @@
     nseg, ncol, order,
     margin_ref, leaf_ref, out_ref, err_ref,
     sblk, lcol, lrow, part, rk, ub, kcol, rp, rm, mb, eb, jb, sq1, sq2,
-    send, lz_r, lx_r, lrow_r, rk_r, ub_r, kz_r, kx_r, row_r, pair_r, m_r, e_r, q1_r, q2_r, local,
+    send, lz_r, lrow_r, rk_r, ub_r, kz_r, kx_r, row_r, pair_r, m_r, e_r, q1_r, q2_r, local,
 ):
     rows, width = leaf_ref.shape
     nx = nseg // 4
@@ -134,13 +135,21 @@
     near = (z - qc <= 1) & (qc - z <= 1)
 
     def pass_on(chosen):
-        for j in range(CHUNKS):
-            block = lcol.at[x, pl.ds(j * step, step)]
-            arrive(chosen & jnp.logical_not(owner), block, lz_r.at[j])
-            push(chosen & (z >= qc) & (z < 3), block, block, lz_r.at[j], seg + nx, col)
-            push(chosen & (z <= qc) & (z > 0), block, block, lz_r.at[j], seg - nx, col)
-            for d in range(1, nx):
-                push(chosen, block, block, lx_r.at[x, j], other_x(d), col)
+        for d in range(nx):
+            slot = jnp.maximum(x - d, 0)
+            held = chosen & (x >= d)
+            for j in range(CHUNKS):
+                block = lcol.at[slot, pl.ds(j * step, step)]
+                if d == 0:
+                    arrive(held & jnp.logical_not(owner), block, lz_r.at[slot, j])
+                else:
+                    arrive(held, block, lz_r.at[slot, j])
+                push(held & (z >= qc) & (z < 3), block, block, lz_r.at[slot, j], seg + nx, col)
+                push(held & (z <= qc) & (z > 0), block, block, lz_r.at[slot, j], seg - nx, col)
+                if d == 0:
+                    for e in range(1, nx):
+                        to_x = lax.rem(x + e, nx)
+                        push(chosen & (owner | (to_x < x)), block, block, lz_r.at[slot, j], other_x(e), col)
 
     pass_on(near)
     fetch.wait()
@@ -158,9 +167,9 @@
             push(x + d < nx, part.at[to_x, here], rk.at[x, here], rk_r.at[x, j], z * nx + to_x, col)
     pass_on(jnp.logical_not(near))
     for d in range(1, nx):
-        from_x = lax.rem(x + d, nx)
+        from_x = jnp.minimum(x + d, nx - 1)
         for j in range(CHUNKS):
-            arrive(None, lcol.at[from_x, pl.ds(j * step, step)], lx_r.at[from_x, j])
+            arrive(x + d < nx, lcol.at[from_x, pl.ds(j * step, step)], lz_r.at[from_x, j])
 
     def form(j):
         here = pl.ds(j * step, step)
@@ -203,10 +212,9 @@
             push(reached & (z < high), block, block, kz_r.at[plane, j], seg + nx, col)
         if not up or distance == 0:
             push(reached & (z > low), block, block, kz_r.at[plane, j], seg - nx, col)
-        if distance < 2:
-            across = None if distance == 0 else reached & jnp.logical_not(same)
-        else:
-            across = reached
+        across = None if distance == 0 else reached
+        if distance == 1 and j < RELAYED:
+            across = reached & jnp.logical_not(same)
         for d in range(1, nx):
             push(across, block, block, kx_r.at[slot, j], other_x(d), col)
 
@@ -226,7 +234,8 @@
             slot = z * nx + lax.rem(x + d, nx)
             block = kcol.at[slot, pl.ds(j * step, step)]
             arrive(None, block, kx_r.at[slot, j])
-            push(None, block, block, kx_r.at[slot, j], sibling * nx + x, col)
+            if j < RELAYED:
+                push(None, block, block, kx_r.at[slot, j], sibling * nx + x, col)
 
     for j in range(CHUNKS):
         form(j)
@@ -384,7 +393,6 @@
             pltpu.VMEM((nseg, 16, 128), F32),
             pltpu.VMEM((ncol, 16, 128), F32),
             dma((SENDS + 16 * nseg,)),
-            dma((CHUNKS,)),
             dma((nx, CHUNKS)),
             dma((cq, CHUNKS)),
             dma((nx, CHUNKS)),

time: 74.8 us -> 66.7 us (0.89)
  Pallas kernels: 70.9 us -> 63 us
    pallas_call x1, Pallas kernels: 70.9 us -> 63 us  [body(): pl.pallas_call(functools.partial(kernel, nseg, ncol, order), out_shape=(j...]
where the time goes in v4:
time: 66.7 us; the launch traced here: 66.5 us
  Pallas kernels  63 us (94%)
  local copies, waits for them, and re-layouts  2.88 us (4%)
    pallas_call x1, Pallas kernels, body(): pl.pallas_call(functools.partial(kernel, nseg, ncol, order), out_shape=(j...  63 us
    unnamed x2, local copies, waits for them, and re-layouts  2.88 us

profile of v4, /device:TPU:0, one launch (start us, length us, event | category | flops | bytes accessed | tf_op | source)
XLA Modules:
  0.0 66.5 jit_solution(17095698239275686852)
XLA Ops:
  0.6 63.0 %shard_map.41 = (f32[192,384]{1,0:T(8,128)}, f32[2]{0:T(128)}) custom-call(f32[192,1536]{1,0:T(8,128)} %margin_ref.1, f32[192,384]{1,0:T(8,128)} %leaf_ref.1), custom_call_target="tpu_custom_call" | custom-call | tf_op jit(solution)/shard_map/pallas_call | solution.py:372
  63.6 1.7 %copy.6 = f32[192,384]{1,0:T(8,128)} copy(f32[192,384]{1,0:T(8,128)} %get-tuple-element.4) | data formatting | bytes 589824
  65.3 1.2 %copy.7 = f32[2]{0:T(128)} copy(f32[2]{0:T(128)} %get-tuple-element.5) | data formatting | bytes 16

commit v5 on v4

--- a/solution.py
+++ b/solution.py
@@ -11,7 +11,7 @@
 F32 = jnp.float32
 CHUNKS = 3
 RELAYED = 1
-SENDS = 128
+SENDS = 192
 
 
 def dot(left, right, left_dim=1):
@@ -109,6 +109,8 @@
     owner = qc == z
     own_slot = lax.rem(col, cq)
 
+    lcol[...] = jnp.zeros_like(lcol)
+
     @pl.when(owner)
     def _():
         lcol[x] = leaf_ref[...]
@@ -134,22 +136,30 @@
             push(lead, block, block, lrow_r.at[k, j], seg, mate)
     near = (z - qc <= 1) & (qc - z <= 1)
 
+    def nonzero(slot, j):
+        first = slot * rows + j * step
+        for place in range(cq):
+            start = max(0, first - place * width) // 128 * 128
+            if start < width:
+                view = lcol.at[slot, pl.ds(j * step, step), pl.ds(start, width - start)]
+                yield own_slot == place, view
+
     def pass_on(chosen):
-        for d in range(nx):
-            slot = jnp.maximum(x - d, 0)
-            held = chosen & (x >= d)
+        for slot in reversed(range(nx)):
+            held = chosen & (x >= slot)
             for j in range(CHUNKS):
-                block = lcol.at[slot, pl.ds(j * step, step)]
-                if d == 0:
-                    arrive(held & jnp.logical_not(owner), block, lz_r.at[slot, j])
-                else:
-                    arrive(held, block, lz_r.at[slot, j])
-                push(held & (z >= qc) & (z < 3), block, block, lz_r.at[slot, j], seg + nx, col)
-                push(held & (z <= qc) & (z > 0), block, block, lz_r.at[slot, j], seg - nx, col)
-                if d == 0:
-                    for e in range(1, nx):
-                        to_x = lax.rem(x + e, nx)
-                        push(chosen & (owner | (to_x < x)), block, block, lz_r.at[slot, j], other_x(e), col)
+                sem = lz_r.at[slot, j]
+                for placed, block in nonzero(slot, j):
+                    use = held & placed
+                    arrive(use & jnp.logical_not(owner & (x == slot)), block, sem)
+                    push(use & (z >= qc) & (z < 3), block, block, sem, seg + nx, col)
+                    push(use & (z <= qc) & (z > 0), block, block, sem, seg - nx, col)
+                    for to_x in range(nx):
+                        if to_x != slot:
+                            cond = use & (x == slot)
+                            if to_x > slot:
+                                cond = cond & owner
+                            push(cond, block, block, sem, z * nx + to_x, col)
 
     pass_on(near)
     fetch.wait()
@@ -166,10 +176,10 @@
             to_x = jnp.minimum(x + d, nx - 1)
             push(x + d < nx, part.at[to_x, here], rk.at[x, here], rk_r.at[x, j], z * nx + to_x, col)
     pass_on(jnp.logical_not(near))
-    for d in range(1, nx):
-        from_x = jnp.minimum(x + d, nx - 1)
+    for slot in range(1, nx):
         for j in range(CHUNKS):
-            arrive(x + d < nx, lcol.at[from_x, pl.ds(j * step, step)], lz_r.at[from_x, j])
+            for placed, block in nonzero(slot, j):
+                arrive((x < slot) & placed, block, lz_r.at[slot, j])
 
     def form(j):
         here = pl.ds(j * step, step)
@@ -392,7 +402,7 @@
             pltpu.VMEM((hc, rows, width), F32),
             pltpu.VMEM((nseg, 16, 128), F32),
             pltpu.VMEM((ncol, 16, 128), F32),
-            dma((SENDS + 16 * nseg,)),
+            dma((SENDS + 24 * nseg,)),
             dma((nx, CHUNKS)),
             dma((cq, CHUNKS)),
             dma((nx, CHUNKS)),

time: 66.7 us -> 65 us (0.975)
  Pallas kernels: 63 us -> 61.3 us
    pallas_call x1, Pallas kernels: 63 us -> 61.3 us  [body(): pl.pallas_call(functools.partial(kernel, nseg, ncol, order), out_shape=(j...]
where the time goes in v5:
time: 65 us; the launch traced here: 64.8 us
  Pallas kernels  61.3 us (94%)
  local copies, waits for them, and re-layouts  2.88 us (4%)
    pallas_call x1, Pallas kernels, body(): pl.pallas_call(functools.partial(kernel, nseg, ncol, order), out_shape=(j...  61.3 us
    unnamed x2, local copies, waits for them, and re-layouts  2.88 us

profile of v5, /device:TPU:0, one launch (start us, length us, event | category | flops | bytes accessed | tf_op | source)
XLA Modules:
  0.0 64.8 jit_solution(15312861735987552474)
XLA Ops:
  0.6 61.3 %shard_map.41 = (f32[192,384]{1,0:T(8,128)}, f32[2]{0:T(128)}) custom-call(f32[192,1536]{1,0:T(8,128)} %margin_ref.1, f32[192,384]{1,0:T(8,128)} %leaf_ref.1), custom_call_target="tpu_custom_call" | custom-call | tf_op jit(solution)/shard_map/pallas_call | solution.py:382
  61.9 1.7 %copy.6 = f32[192,384]{1,0:T(8,128)} copy(f32[192,384]{1,0:T(8,128)} %get-tuple-element.4) | data formatting | bytes 589824
  63.6 1.2 %copy.7 = f32[2]{0:T(128)} copy(f32[2]{0:T(128)} %get-tuple-element.5) | data formatting | bytes 16

commit v6 on v5

--- a/solution.py
+++ b/solution.py
@@ -12,16 +12,6 @@
 CHUNKS = 3
 RELAYED = 1
 SENDS = 192
-
-
-def dot(left, right, left_dim=1):
-    return lax.dot_general(
-        left,
-        right,
-        (((left_dim,), (0,)), ((), ())),
-        precision=lax.Precision.HIGHEST,
-        preferred_element_type=F32,
-    )
 
 
 def parts(values):
@@ -49,11 +39,11 @@
 
 def kernel(
     nseg, ncol, order,
-    margin_ref, leaf_ref, out_ref, err_ref,
-    sblk, lcol, lrow, part, rk, ub, kcol, rp, rm, mb, eb, jb, sq1, sq2,
+    margin_ref, leaf_hbm, out_ref, err_ref,
+    leaf_ref, sblk, lcol, lrow, part, rk, ub, kcol, rp, rm, mb, eb, jb, sq1, sq2,
     send, lz_r, lrow_r, rk_r, ub_r, kz_r, kx_r, row_r, pair_r, m_r, e_r, q1_r, q2_r, local,
 ):
-    rows, width = leaf_ref.shape
+    rows, width = leaf_hbm.shape
     nx = nseg // 4
     cq = ncol // 4
     hs, hc = nseg // 2, ncol // 2
@@ -110,17 +100,20 @@
     own_slot = lax.rem(col, cq)
 
     lcol[...] = jnp.zeros_like(lcol)
-
-    @pl.when(owner)
-    def _():
-        lcol[x] = leaf_ref[...]
-        lrow[own_slot] = leaf_ref[...]
-
     barrier = pltpu.get_barrier_semaphore()
     for d in range(1, nseg):
         pl.semaphore_signal(barrier, inc=1, device_id=(lax.rem(seg + d, nseg), col), device_id_type=MESH)
     for d in range(1, ncol):
         pl.semaphore_signal(barrier, inc=1, device_id=(seg, lax.rem(col + d, ncol)), device_id_type=MESH)
+    load = pltpu.make_async_copy(leaf_hbm, leaf_ref, local.at[1])
+    load.start()
+    load.wait()
+
+    @pl.when(owner)
+    def _():
+        lrow[own_slot] = leaf_ref[...]
+        lcol[x] = leaf_ref[...]
+
     pl.semaphore_wait(barrier, nseg + ncol - 2)
 
     mate = col + 1 - 2 * lax.rem(col, 2)
@@ -168,7 +161,7 @@
             lead = lax.rem(col, 2) == lax.rem(z * cq + k, 2)
             arrive(jnp.logical_not(lead), lrow.at[k, pl.ds(j * step, step)], lrow_r.at[k, j])
     for k in range(cq):
-        piece = dot(lrow[k], sblk[...], 0)
+        piece = dot3(lrow[k].T, sblk[...])
         part[pl.ds(k * per, per)] = piece.reshape(per, rows, width)
     for j in range(CHUNKS):
         here = pl.ds(j * step, step)
@@ -201,7 +194,7 @@
             arrive(None, ub.at[k, here], ub_r.at[k, j])
         total = None
         for k in range(cq):
-            term = dot(ub[k, here], lcol[pl.ds(k * per, per)].reshape(width, width))
+            term = dot3(ub[k, here], lcol[pl.ds(k * per, per)].reshape(width, width))
             total = term if total is None else total + term
         kcol[seg, here] = total
 
@@ -305,11 +298,8 @@
     from_siblings(diag, mb, m_r, 0)
 
     def product(buf, half):
-        total = None
-        for k in range(hc):
-            term = dot3(buf[k], kcol[pl.ds(half * hs + k * per, per)].reshape(width, width))
-            total = term if total is None else total + term
-        return total
+        left = jnp.concatenate([buf[k] for k in range(hc)], axis=1)
+        return dot3(left, kcol[pl.ds(half * hs, hs)].reshape(hs * rows, width))
 
     @pl.when(diag)
     def _():
@@ -385,9 +375,10 @@
             jax.ShapeDtypeStruct((rows, width), F32),
             jax.ShapeDtypeStruct((2,), F32),
         ),
-        in_specs=[pl.BlockSpec(memory_space=pl.ANY), pl.BlockSpec(memory_space=pltpu.VMEM)],
+        in_specs=[pl.BlockSpec(memory_space=pl.ANY)] * 2,
         out_specs=(pl.BlockSpec(memory_space=pltpu.VMEM), pl.BlockSpec(memory_space=pltpu.SMEM)),
         scratch_shapes=[
+            pltpu.VMEM((rows, width), F32),
             pltpu.VMEM((rows, width), F32),
             pltpu.VMEM((nx, rows, width), F32),
             pltpu.VMEM((cq, rows, width), F32),
@@ -415,7 +406,7 @@
             dma((2, hc)),
             dma((nseg,)),
             dma((ncol,)),
-            dma((1,)),
+            dma((2,)),
         ],
         compiler_params=pltpu.CompilerParams(
             collective_id=0, has_side_effects=True, vmem_limit_bytes=56 * 1024 * 1024

time: 65 us -> 63.3 us (0.974)
  Pallas kernels: 61.3 us -> 59.6 us
    pallas_call x1, Pallas kernels: 61.3 us -> 59.6 us  [body(): pl.pallas_call(functools.partial(kernel, nseg, ncol, order), out_shape=(j...]
where the time goes in v6:
time: 63.3 us; the launch traced here: 63.1 us
  Pallas kernels  59.6 us (94%)
  local copies, waits for them, and re-layouts  2.88 us (5%)
  between operations  0.64 us (1%)
    pallas_call x1, Pallas kernels, body(): pl.pallas_call(functools.partial(kernel, nseg, ncol, order), out_shape=(j...  59.6 us
    unnamed x2, local copies, waits for them, and re-layouts  2.88 us

profile of v6, /device:TPU:0, one launch (start us, length us, event | category | flops | bytes accessed | tf_op | source)
XLA Modules:
  0.0 63.1 jit_solution(17531556435138923401)
XLA Ops:
  0.6 59.6 %shard_map.41 = (f32[192,384]{1,0:T(8,128)}, f32[2]{0:T(128)}) custom-call(f32[192,1536]{1,0:T(8,128)} %margin_ref.1, f32[192,384]{1,0:T(8,128)} %leaf_hbm.1), custom_call_target="tpu_custom_call" | custom-call | tf_op jit(solution)/shard_map/pallas_call | solution.py:372
  60.2 1.7 %copy.6 = f32[192,384]{1,0:T(8,128)} copy(f32[192,384]{1,0:T(8,128)} %get-tuple-element.4) | data formatting | bytes 589824
  61.9 1.2 %copy.7 = f32[2]{0:T(128)} copy(f32[2]{0:T(128)} %get-tuple-element.5) | data formatting | bytes 16

commit v7 on v6

--- a/solution.py
+++ b/solution.py
@@ -10,8 +10,9 @@
 MESH = pl.DeviceIdType.MESH
 F32 = jnp.float32
 CHUNKS = 3
-RELAYED = 1
-SENDS = 192
+PIECES = 6
+RELAYED = 2
+SENDS = 256
 
 
 def parts(values):
@@ -50,6 +51,7 @@
     per = width // rows
     quarter = nx * rows
     step = rows // CHUNKS
+    size = rows // PIECES
 
     seg = lax.axis_index("seg")
     col = lax.axis_index("col")
@@ -208,12 +210,12 @@
         high = jnp.where(wide, 3, 2 * hseg + 1)
         plane = jnp.clip(origin, 0, 3)
         slot = plane * nx + x
-        block = kcol.at[slot, pl.ds(j * step, step)]
+        block = kcol.at[slot, pl.ds(j * size, size)]
         if distance:
             arrive(reached, block, kz_r.at[plane, j])
-        if up or distance == 0:
+        if distance < 3 and (up or distance == 0):
             push(reached & (z < high), block, block, kz_r.at[plane, j], seg + nx, col)
-        if not up or distance == 0:
+        if distance < 3 and not up:
             push(reached & (z > low), block, block, kz_r.at[plane, j], seg - nx, col)
         across = None if distance == 0 else reached
         if distance == 1 and j < RELAYED:
@@ -229,20 +231,21 @@
         reached = valid & (same if inside else wide & jnp.logical_not(same))
         for d in range(1, nx):
             slot = jnp.clip(origin, 0, 3) * nx + lax.rem(x + d, nx)
-            arrive(reached, kcol.at[slot, pl.ds(j * step, step)], kx_r.at[slot, j])
+            arrive(reached, kcol.at[slot, pl.ds(j * size, size)], kx_r.at[slot, j])
 
     def relay(j):
         sibling = 2 * hseg + 1 - lax.rem(z, 2)
         for d in range(1, nx):
             slot = z * nx + lax.rem(x + d, nx)
-            block = kcol.at[slot, pl.ds(j * step, step)]
+            block = kcol.at[slot, pl.ds(j * size, size)]
             arrive(None, block, kx_r.at[slot, j])
             if j < RELAYED:
                 push(None, block, block, kx_r.at[slot, j], sibling * nx + x, col)
 
     for j in range(CHUNKS):
         form(j)
-        spread(0, False, j)
+        for piece in range(j * PIECES // CHUNKS, (j + 1) * PIECES // CHUNKS):
+            spread(0, False, piece)
 
     partner = lax.rem(col + hc, ncol)
     row_ids = seg * rows + lax.broadcasted_iota(jnp.int32, (rows, width), 0)
@@ -273,10 +276,10 @@
     siblings(diag, rp, row_r, 0)
 
     off = jnp.logical_not(diag)
-    for j in range(CHUNKS):
+    for j in range(PIECES):
         spread(1, True, j)
         spread(1, False, j)
-    for j in range(CHUNKS):
+    for j in range(PIECES):
         relay(j)
         spread(2, True, j)
         spread(2, False, j)
@@ -292,7 +295,7 @@
         mb[mine] = 1.5 * leaf_ref[...] - 0.5 * update
 
     siblings(diag, mb, m_r, 0)
-    for j in range(CHUNKS):
+    for j in range(PIECES):
         settle(1, True, j, True)
         settle(1, False, j, True)
     from_siblings(diag, mb, m_r, 0)
@@ -311,7 +314,7 @@
     from_siblings(None, rp, row_r, 0)
     eb[mine] = product(rp, hseg)
     siblings(None, eb, e_r, 0)
-    for j in range(CHUNKS):
+    for j in range(PIECES):
         spread(3, True, j)
         spread(3, False, j)
 
@@ -322,7 +325,7 @@
     siblings(None, jb, e_r, 1)
 
     for distance in (1, 2, 3):
-        for j in range(CHUNKS):
+        for j in range(PIECES):
             settle(distance, True, j, False)
             settle(distance, False, j, False)
     from_siblings(None, eb, e_r, 0)
@@ -393,13 +396,13 @@
             pltpu.VMEM((hc, rows, width), F32),
             pltpu.VMEM((nseg, 16, 128), F32),
             pltpu.VMEM((ncol, 16, 128), F32),
-            dma((SENDS + 24 * nseg,)),
+            dma((SENDS + 32 * nseg,)),
             dma((nx, CHUNKS)),
             dma((cq, CHUNKS)),
             dma((nx, CHUNKS)),
             dma((cq, CHUNKS)),
-            dma((4, CHUNKS)),
-            dma((nseg, CHUNKS)),
+            dma((4, PIECES)),
+            dma((nseg, PIECES)),
             dma((2, hc)),
             dma((2,)),
             dma((1, hc)),

time: 63.3 us -> 64.8 us (1.024)
  Pallas kernels: 59.6 us -> 61.1 us
    pallas_call x1, Pallas kernels: 59.6 us -> 61.1 us  [body(): pl.pallas_call(functools.partial(kernel, nseg, ncol, order), out_shape=(j...]
where the time goes in v7:
time: 64.8 us; the launch traced here: 64.6 us
  Pallas kernels  61.1 us (94%)
  local copies, waits for them, and re-layouts  2.88 us (4%)
    pallas_call x1, Pallas kernels, body(): pl.pallas_call(functools.partial(kernel, nseg, ncol, order), out_shape=(j...  61.1 us
    unnamed x2, local copies, waits for them, and re-layouts  2.88 us

profile of v7, /device:TPU:0, one launch (start us, length us, event | category | flops | bytes accessed | tf_op | source)
XLA Modules:
  0.0 64.6 jit_solution(16897755586648847448)
XLA Ops:
  0.6 61.1 %shard_map.41 = (f32[192,384]{1,0:T(8,128)}, f32[2]{0:T(128)}) custom-call(f32[192,1536]{1,0:T(8,128)} %margin_ref.1, f32[192,384]{1,0:T(8,128)} %leaf_hbm.1), custom_call_target="tpu_custom_call" | custom-call | tf_op jit(solution)/shard_map/pallas_call | solution.py:375
  61.7 1.7 %copy.6 = f32[192,384]{1,0:T(8,128)} copy(f32[192,384]{1,0:T(8,128)} %get-tuple-element.4) | data formatting | bytes 589824
  63.4 1.2 %copy.7 = f32[2]{0:T(128)} copy(f32[2]{0:T(128)} %get-tuple-element.5) | data formatting | bytes 16

commit v8 on v7

--- a/solution.py
+++ b/solution.py
@@ -9,9 +9,9 @@
 
 MESH = pl.DeviceIdType.MESH
 F32 = jnp.float32
-CHUNKS = 3
-PIECES = 6
-RELAYED = 2
+CHUNKS = 2
+PIECES = 2
+RELAYED = 1
 SENDS = 256
 
 
@@ -365,6 +365,14 @@
             copy.wait_send()
         else:
             pl.when(cond)(copy.wait_send)
+
+
+def hand_on(factor_in, err_in, factor_out, err_out, sem):
+    copy = pltpu.make_async_copy(factor_in, factor_out, sem)
+    copy.start()
+    for level in range(2):
+        err_out[level] = err_in[level]
+    copy.wait()
 
 
 def body(nseg, ncol, margin, leaf_factor):
@@ -415,7 +423,13 @@
             collective_id=0, has_side_effects=True, vmem_limit_bytes=56 * 1024 * 1024
         ),
     )(margin, leaf_factor)
-    return factor, errors
+    return pl.pallas_call(
+        hand_on,
+        out_shape=(jax.ShapeDtypeStruct((rows, width), F32), jax.ShapeDtypeStruct((2,), F32)),
+        in_specs=[pl.BlockSpec(memory_space=pl.ANY), pl.BlockSpec(memory_space=pltpu.SMEM)],
+        out_specs=(pl.BlockSpec(memory_space=pl.ANY), pl.BlockSpec(memory_space=pltpu.SMEM)),
+        scratch_shapes=[pltpu.SemaphoreType.DMA],
+    )(factor, errors)
 
 
 def solution(mesh):

time: 64.8 us -> 76.1 us (1.17)
  Pallas kernels: 61.1 us -> 75.3 us
  local copies, waits for them, and re-layouts: 2.88 us -> 0 us
    pallas_call x0 -> x1, Pallas kernels: none -> 11.2 us  [body(): pl.pallas_call(hand_on, out_shape=(jax.ShapeDtypeStruct((rows, width), F3...]
    pallas_call x1, Pallas kernels: 61.1 us -> 64.1 us  [body(): pl.pallas_call(functools.partial(kernel, nseg, ncol, order), out_shape=(j...]
    unnamed x2 -> x0, local copies, waits for them, and re-layouts: 2.88 us -> none
where the time goes in v8:
time: 76.1 us; the launch traced here: 75.9 us
  Pallas kernels  75.3 us (99%)
    pallas_call x1, Pallas kernels, body(): pl.pallas_call(functools.partial(kernel, nseg, ncol, order), out_shape=(j...  64.1 us
    pallas_call x1, Pallas kernels, body(): pl.pallas_call(hand_on, out_shape=(jax.ShapeDtypeStruct((rows, width), F3...  11.2 us

profile of v8, /device:TPU:0, one launch (start us, length us, event | category | flops | bytes accessed | tf_op | source)
XLA Modules:
  0.0 75.9 jit_solution(12706221549622981524)
XLA Ops:
  0.6 64.1 %shard_map.41 = (f32[192,384]{1,0:T(8,128)}, f32[2]{0:T(128)}) custom-call(f32[192,1536]{1,0:T(8,128)} %margin_ref.1, f32[192,384]{1,0:T(8,128)} %leaf_hbm.1), custom_call_target="tpu_custom_call" | custom-call | tf_op jit(solution)/shard_map/pallas_call | solution.py:383
  64.7 11.2 %shard_map.42 = (f32[192,384]{1,0:T(8,128)}, f32[2]{0:T(128)}) custom-call(f32[192,384]{1,0:T(8,128)} %get-tuple-element.4.factor_in, f32[2]{0:T(128)} %get-tuple-element.5.err_in), custom_call_target="tpu_custom_call" | custom-call | tf_op jit(solution)/shard_map/pallas_call | solution.py:426

commit v9 on v7

--- a/solution.py
+++ b/solution.py
@@ -10,8 +10,8 @@
 MESH = pl.DeviceIdType.MESH
 F32 = jnp.float32
 CHUNKS = 3
-PIECES = 6
-RELAYED = 2
+PIECES = 3
+RELAYED = 0
 SENDS = 256
 
 
@@ -365,6 +365,12 @@
             copy.wait_send()
         else:
             pl.when(cond)(copy.wait_send)
+
+
+def hand_on(factor_in, err_in, factor_out, err_out):
+    factor_out[...] = factor_in[...]
+    for level in range(2):
+        err_out[level] = err_in[level]
 
 
 def body(nseg, ncol, margin, leaf_factor):
@@ -415,7 +421,12 @@
             collective_id=0, has_side_effects=True, vmem_limit_bytes=56 * 1024 * 1024
         ),
     )(margin, leaf_factor)
-    return factor, errors
+    return pl.pallas_call(
+        hand_on,
+        out_shape=(jax.ShapeDtypeStruct((rows, width), F32), jax.ShapeDtypeStruct((2,), F32)),
+        in_specs=[pl.BlockSpec(memory_space=pltpu.VMEM), pl.BlockSpec(memory_space=pltpu.SMEM)],
+        out_specs=(pl.BlockSpec(memory_space=pltpu.VMEM), pl.BlockSpec(memory_space=pltpu.SMEM)),
+    )(factor, errors)
 
 
 def solution(mesh):

time: 64.8 us -> 63 us (0.972)
  local copies, waits for them, and re-layouts: 2.88 us -> 0 us
  Pallas kernels: 61.1 us -> 61.9 us
    unnamed x2 -> x0, local copies, waits for them, and re-layouts: 2.88 us -> none
    pallas_call x0 -> x1, Pallas kernels: none -> 1.71 us  [body(): pl.pallas_call(hand_on, out_shape=(jax.ShapeDtypeStruct((rows, width), F3...]
    pallas_call x1, Pallas kernels: 61.1 us -> 60.2 us  [body(): pl.pallas_call(functools.partial(kernel, nseg, ncol, order), out_shape=(j...]
where the time goes in v9:
time: 63 us; the launch traced here: 62.6 us
  Pallas kernels  61.9 us (98%)
  between operations  0.64 us (1%)
    pallas_call x1, Pallas kernels, body(): pl.pallas_call(functools.partial(kernel, nseg, ncol, order), out_shape=(j...  60.2 us
    pallas_call x1, Pallas kernels, body(): pl.pallas_call(hand_on, out_shape=(jax.ShapeDtypeStruct((rows, width), F3...  1.71 us

profile of v9, /device:TPU:0, one launch (start us, length us, event | category | flops | bytes accessed | tf_op | source)
XLA Modules:
  0.0 62.6 jit_solution(4611968756840845698)
XLA Ops:
  0.6 60.2 %shard_map.41 = (f32[192,384]{1,0:T(8,128)}, f32[2]{0:T(128)}) custom-call(f32[192,1536]{1,0:T(8,128)} %margin_ref.1, f32[192,384]{1,0:T(8,128)} %leaf_hbm.1), custom_call_target="tpu_custom_call" | custom-call | tf_op jit(solution)/shard_map/pallas_call | solution.py:381
  60.9 1.7 %shard_map.42 = (f32[192,384]{1,0:T(8,128)}, f32[2]{0:T(128)}) custom-call(f32[192,384]{1,0:T(8,128)} %get-tuple-element.4.factor_in, f32[2]{0:T(128)} %get-tuple-element.5.err_in), custom_call_target="tpu_custom_call" | custom-call | tf_op jit(solution)/shard_map/pallas_call | solution.py:424
